TPU v7x, 32 devices: a whole 2x2x4 slice. The times are simulated.
32 devices in a mesh: space: 8 (over z, x), probe: 4 (over y, core).
Axes of the slice: x: 2, y: 2, z: 4, core: 2. Of those that a mesh axis runs over, the one named last changes fastest.
Arguments:
- probes: float32 [128, 16, 128, 128], P('probe', 'space'), may hold values from -20 to 20, as said below
- winds: float32 [4, 3, 16, 128, 128], P(None, None, 'space'), may hold values from -0.12 to 0.12
- wind_step: int32 [16], P('space'), may hold values from 0 to 3
- obs_weight: float32 [16, 128, 128], P('space'), may hold values from 0.5 to 6, as said below
- prior_weight: float32 [16, 128, 128], P('space'), may hold values from 0.2 to 3, as said below
Outputs:
- basis_out: float32 [128, 16, 128, 128], P(None, 'space', 'probe')
- r_factor: float32 [128, 128], replicated
Inputs may be any that keep to these rules, and one draw needn't show every extreme that they name: `probes`: probe vectors of unlike scales with parts in common between them. `obs_weight`: positive. `prior_weight`: positive.
All inputs are finite; a program needn't handle non-finite values.
Results may differ from a plain program's by a relative error of at most 0.00011.
Values sent between devices are 32-bit elements; how exact they have to be, the bound alone decides.
A program may use at most 128 MiB of HBM per device.

v0:
```python
import math

import jax
import jax.numpy as jnp
from jax import lax
from jax.sharding import PartitionSpec as P

diffusion = 0.1


def extended(block, sides, width):
    for axis, dim in sides:
        count = lax.axis_size(axis)
        forward = [(i, i + 1) for i in range(count - 1)]
        backward = [(target, source) for source, target in forward]
        low = lax.ppermute(
            lax.slice_in_dim(block, block.shape[dim] - width, None, axis=dim), axis, forward
        )
        high = lax.ppermute(lax.slice_in_dim(block, 0, width, axis=dim), axis, backward)
        block = jnp.concatenate([low, block, high], axis=dim)
    return block


def window_cut(array_in, axis_dim, offset):
    leading = array_in.ndim - 3
    result_cut = array_in
    for spatial in range(3):
        shift_now = offset if spatial == axis_dim else 0
        length_dim = array_in.shape[leading + spatial] - 2
        result_cut = lax.slice_in_dim(
            result_cut, 1 + shift_now, 1 + shift_now + length_dim, axis=leading + spatial
        )
    return result_cut


def stencil(values_pad, wind_pad, transposed):
    centre = window_cut(values_pad, 0, 0)
    result_sum = centre
    for axis_dim in range(3):
        next_cells = window_cut(values_pad, axis_dim, 1)
        prev_cells = window_cut(values_pad, axis_dim, -1)
        speed_now = window_cut(wind_pad[axis_dim], axis_dim, 0)
        speed_pos = jnp.maximum(speed_now, 0.0)
        speed_neg = jnp.minimum(speed_now, 0.0)
        if transposed:
            pos_next = jnp.maximum(window_cut(wind_pad[axis_dim], axis_dim, 1), 0.0)
            neg_prev = jnp.minimum(window_cut(wind_pad[axis_dim], axis_dim, -1), 0.0)
            result_sum = (
                result_sum
                - speed_pos * centre
                + pos_next * next_cells
                + speed_neg * centre
                - neg_prev * prev_cells
            )
        else:
            result_sum = (
                result_sum - speed_pos * (centre - prev_cells) - speed_neg * (next_cells - centre)
            )
        result_sum = result_sum + diffusion * (next_cells - 2.0 * centre + prev_cells)
    return result_sum


def pad_trailing(array_in):
    widths = [(0, 0)] * array_in.ndim
    widths[-1] = (1, 1)
    widths[-2] = (1, 1)
    return jnp.pad(array_in, widths)


def select_wind(winds, wind_step):
    levels = jnp.arange(winds.shape[0], dtype=jnp.int32)
    picked = levels[:, None] == wind_step[None, :]
    return jnp.sum(jnp.where(picked[:, None, :, None, None], winds, jnp.zeros_like(winds)), axis=0)


def per_device(probes, winds, wind_step, obs_weight, prior_weight):
    wind_now = select_wind(winds, wind_step)
    wind_x = extended(wind_now, (("space", 1),), 1)
    wind_pad = pad_trailing(wind_x)
    values_pad = pad_trailing(extended(probes, (("space", 1),), 1))
    weighted = obs_weight * stencil(values_pad, wind_pad, False)
    weighted_pad = pad_trailing(extended(weighted, (("space", 1),), 1))
    hess_full = stencil(weighted_pad, wind_pad, True) + prior_weight * probes
    hess_image = lax.all_to_all(hess_full, "probe", split_axis=2, concat_axis=0, tiled=True)
    row_block = hess_image.reshape(hess_image.shape[0], -1)
    gram_local = lax.dot_general(
        row_block,
        row_block,
        (((1,), (1,)), ((), ())),
        precision=lax.Precision.HIGHEST,
        preferred_element_type=jnp.float32,
    )
    low_factor = jnp.linalg.cholesky(lax.psum(gram_local, ("space", "probe")))
    cells_all = row_block.shape[1] * lax.axis_size("space") * lax.axis_size("probe")
    norm_scale = math.sqrt(cells_all)
    solved = jax.scipy.linalg.solve_triangular(low_factor, row_block, lower=True)
    basis_out = (solved * norm_scale).reshape(hess_image.shape)
    return (basis_out, low_factor.T / norm_scale)


def solution(mesh):
    placed = (
        P("probe", "space", None, None),
        P(None, None, "space", None, None),
        P("space"),
        P("space", None, None),
        P("space", None, None),
    )
    return jax.shard_map(
        per_device,
        mesh=mesh,
        in_specs=placed,
        out_specs=(P(None, "space", "probe", None), P()),
        check_vma=False,
    )
```

profile of v0, /device:TPU:0, one launch (start us, length us, event | category | flops | bytes accessed | tf_op | source)
XLA Modules:
  0.0 494.4 jit_solution(12243450868694497816)
XLA Ops:
  7.2 0.0 copy-start.11
  7.2 0.0 copy-start.6
  7.2 0.0 all-reduce.5.cloned.1.call-start
  7.2 2.8 fusion.46
  10.1 5.0 %collective-permute-start.2 = (f32[32,1,128,128]{3,2,1,0:T(8,128)S(1)}, f32[32,1,128,128]{3,2,1,0:T(8,128)S(1)}, u32[]{:S(2)}, u32[]{:S(2)}) collective-permute-start(f32[32,1,128,128]{3,2,1,0:T(8,128)S(1)} %get-tuple-element.12), channel_id=1, source_target_pairs={{0,4},{4,8},{8,12},{12,16},{16,20},{20,24},{24,28},{1,5},{5,9},{9,... | collective-permute-start | bytes 6291464 | tf_op jit(solution)/shard_map/ppermute | solution.py:16
  15.1 1.3 collective-permute-start.3
  16.4 0.0 copy-done.11
  16.4 0.0 copy-done.6
  16.4 0.2 select_reduce_fusion
  16.6 0.0 copy-start
  16.6 4.8 collective-permute-start
  21.5 1.3 collective-permute-start.1
  22.8 90.4 %collective-permute-done = f32[3,1,128,128]{3,2,1,0:T(8,128)S(1)} collective-permute-done((f32[3,1,128,128]{3,2,1,0:T(8,128)S(1)}, f32[3,1,128,128]{3,2,1,0:T(8,128)S(1)}, u32[]{:S(2)}, u32[]{:S(2)}) %collective-permute-start) | collective-permute-done | bytes 196640 | tf_op jit(solution)/shard_map/ppermute | solution.py:16
  113.2 0.0 collective-permute-done.1
  113.2 0.5 select_maximum_fusion.4
  113.7 1.0 slice_bitcast_fusion.1
  114.7 0.1 slice_maximum_fusion.5
  114.8 0.9 slice_maximum_fusion
  115.7 0.0 collective-permute-done.2
  115.7 0.0 copy-start.4
  115.7 0.0 collective-permute-done.3
  115.7 0.0 copy-done
  115.7 0.0 copy-start.5
  115.7 14.0 %select_maximum_fusion.2 = f32[32,4,130,130]{3,2,1,0:T(8,128)} fusion(f32[32,1,128,128]{3,2,1,0:T(8,128)S(1)} %collective-permute-done.3, f32[32,2,128,128]{3,2,1,0:T(8,128)S(1)} %copy-done, f32[32,1,128,128]{3,2,1,0:T(8,128)S(1)} %collective-permute-done.2), kind=kLoop, calls=%fused_computation.6 | loop fusion | flops 32448000 | bytes 17041408 | tf_op jit(solution)/shard_map/concatenate | solution.py:20
  129.8 0.0 copy-done.4
  129.8 0.0 copy-done.5
  129.8 16.5 %fusion.29 = f32[32,2,128,128]{3,2,1,0:T(8,128)} fusion(f32[32,1,128,128]{3,2,1,0:T(8,128)} %copy-done.5, f32[32,2,128,128]{3,2,1,0:T(8,128)S(1)} %copy-done, f32[32,1,128,128]{3,2,1,0:T(8,128)} %copy-done.4, f32[32,4,130,130]{3,2,1,0:T(8,128)} %select_maximum_fusion.2, f32[2,128,128]{2,1,0:T(8,128)S(1)} %get-tuple-element.26, ...), kind=kLoop, calls=%fused_computation.42 | loop fusion | flops 35651584 | bytes 30277632 | tf_op jit(solution)/shard_map/mul | solution.py:81
  146.3 0.0 copy-start.1
  146.3 2.6 fusion.45
  148.9 4.5 collective-permute-start.5
  153.4 1.5 collective-permute-start.4
  154.9 1.2 slice_minimum_fusion.2
  156.1 0.0 copy-start.7
  156.1 0.0 copy-start.8
  156.1 0.0 copy-start.9
  156.1 0.0 copy-start.10
  156.1 86.1 %collective-permute-done.5 = f32[32,1,128,128]{3,2,1,0:T(8,128)S(1)} collective-permute-done((f32[32,1,128,128]{3,2,1,0:T(8,128)S(1)}, f32[32,1,128,128]{3,2,1,0:T(8,128)S(1)}, u32[]{:S(2)}, u32[]{:S(2)}) %collective-permute-start.5) | collective-permute-done | bytes 2097184 | tf_op jit(solution)/shard_map/ppermute | solution.py:16
  242.2 0.0 copy-start.2
  242.2 0.0 collective-permute-done.4
  242.2 0.0 copy-done.1
  242.3 7.6 %select_maximum_fusion = f32[32,4,130,130]{3,2,1,0:T(8,128)S(1)} fusion(f32[32,1,128,128]{3,2,1,0:T(8,128)S(1)} %collective-permute-done.4, f32[32,2,128,128]{3,2,1,0:T(8,128)S(1)} %copy-done.1, f32[32,1,128,128]{3,2,1,0:T(8,128)S(1)} %collective-permute-done.5), kind=kLoop, calls=%fused_computation.4 | loop fusion | flops 32448000 | bytes 17041408 | tf_op jit(solution)/shard_map/concatenate | solution.py:20
  249.8 0.0 copy-done.2
  249.8 0.0 copy-done.3
  249.8 0.0 copy-done.7
  249.9 0.0 copy-done.8
  249.9 0.0 copy-done.9
  249.9 0.0 copy-done.10
  249.9 10.8 %fusion.17 = f32[32,2,128,128]{3,2,1,0:T(8,128)} fusion(f32[32,2,128,128]{3,2,1,0:T(8,128)} %fusion.29, f32[32,2,128,128]{3,2,1,0:T(8,128)S(1)} %copy-done, f32[32,4,130,130]{3,2,1,0:T(8,128)S(1)} %select_maximum_fusion, f32[32,1,128,128]{3,2,1,0:T(8,128)} %copy-done.2, f32[32,1,128,128]{3,2,1,0:T(8,128)} %copy-done.3, f32[2,128,128]{2,1,0:T(8,128)S(1)} %copy-done.10, ...), kind=kLoop, calls=%fused_computation.27 | loop fusion | flops 42991616 | bytes 35258368 | tf_op jit(solution)/shard_map/add | solution.py:83
  260.7 4.6 copy.34
  265.3 50.8 %all_to_all.15 = f32[32,2,128,128]{3,0,1,2:T(8,128)S(1)} all-to-all(f32[32,2,128,128]{3,0,1,2:T(8,128)S(1)} %copy.34), channel_id=1, replica_groups=mesh['space'=8,'probe'=4] {'probe'}, dimensions={2} | all-to-all | bytes 8388608 | tf_op jit(solution)/shard_map/all_to_all | solution.py:84
  316.1 4.4 copy.42
  320.5 5.0 %reshape.58 = f32[128,8192]{1,0:T(8,128)} reshape(f32[4,32,2,32,128]{4,3,2,1,0:T(8,128)} %bitcast.35) | data formatting | bytes 8388608 | tf_op jit(solution)/shard_map/reshape | solution.py:85
  325.5 7.6 %fusion.48 = f32[128,128]{0,1:T(8,128)} fusion(f32[128,8192]{1,0:T(8,128)} %reshape.58), kind=kOutput, calls=%fused_computation.98 | convolution fusion | flops 1610612736 | bytes 4259840 | tf_op jit(solution)/shard_map/dot_general | solution.py:86
  333.1 0.0 all-reduce.5.cloned.1.call-update
  333.1 120.9 %all-reduce.5.cloned.1.call-done = f32[128,128]{0,1:T(8,128)} async-done(((f32[128,128]{0,1:T(8,128)}), f32[128,128]{0,1:T(8,128)}) %all-reduce.5.cloned.1.call-update) | async-done | bytes 65552 | tf_op jit(solution)/shard_map/psum | solution.py:93
  454.0 0.9 copy.37
  454.9 0.9 fusion.44
  455.8 11.7 %cholesky.16 = f32[128,128]{1,0:T(8,128)S(1)} custom-call(f32[128,128]{1,0:T(8,128)S(1)} %fusion.44), custom_call_target="Cholesky" | custom-call | tf_op jit(solution)/shard_map/jit(cholesky)/cholesky | solution.py:93
  467.5 0.6 compare_reduce_fusion
  468.2 0.7 multiply_bitcast_fusion
  468.8 0.7 copy.38
  469.6 9.8 %custom-call.7 = f32[1,128,128]{1,2,0:T(8,128)S(1)} custom-call(f32[1,128,128]{2,1,0:T(8,128)S(1)} %get-tuple-element.32), custom_call_target="InvertDiagBlocksLowerTriangular" | custom-call | tf_op jit(solution)/shard_map/jit(_solve_triangular)/triangular_solve | solution.py:96
  479.4 5.4 %fusion.39 = f32[16,8,64,128]{3,1,2,0:T(8,128)S(1)} fusion(f32[128,8192]{1,0:T(8,128)} %reshape.58, f32[1,128,128]{1,2,0:T(8,128)S(1)} %custom-call.7), kind=kOutput, calls=%fused_computation.60 | convolution fusion | flops 1611661312 | bytes 8454144 | tf_op jit(solution)/shard_map/jit(_solve_triangular)/triangular_solve | solution.py:96
  484.8 2.8 copy.40
  (4 shorter events, 0.1 us)
Async XLA Ops:
  7.2 9.2 %copy-start.11 = (s32[2]{0:T(128)S(1)}, s32[2]{0:T(128)}, u32[]{:S(2)}) copy-start(s32[2]{0:T(128)} %param.7) | copy-start | bytes 28
  7.2 9.2 %copy-start.6 = (f32[4,3,2,128,128]{4,3,2,1,0:T(8,128)S(1)}, f32[4,3,2,128,128]{4,3,2,1,0:T(8,128)}, u32[]{:S(2)}) copy-start(f32[4,3,2,128,128]{4,3,2,1,0:T(8,128)} %param.6) | copy-start | bytes 4718596
  7.2 446.8 %all-reduce.5.cloned.1.call-start = ((), (), s32[]{:S(2)}) async-start(), calls=%async_computation.1 | async-start | bytes 131072 | tf_op jit(solution)/shard_map/psum | solution.py:93
  10.1 105.6 %collective-permute-start.2 = (f32[32,1,128,128]{3,2,1,0:T(8,128)S(1)}, f32[32,1,128,128]{3,2,1,0:T(8,128)S(1)}, u32[]{:S(2)}, u32[]{:S(2)}) collective-permute-start(f32[32,1,128,128]{3,2,1,0:T(8,128)S(1)} %get-tuple-element.12), channel_id=1, source_target_pairs={{0,4},{4,8},{8,12},{12,16},{16,20},{20,24},{24,28},{1,5},{5,9},{9,... | collective-permute-start | bytes 6291464 | tf_op jit(solution)/shard_map/ppermute | solution.py:16
  15.1 100.7 %collective-permute-start.3 = (f32[32,1,128,128]{3,2,1,0:T(8,128)S(1)}, f32[32,1,128,128]{3,2,1,0:T(8,128)S(1)}, u32[]{:S(2)}, u32[]{:S(2)}) collective-permute-start(f32[32,1,128,128]{3,2,1,0:T(8,128)S(1)} %get-tuple-element.13), channel_id=1, source_target_pairs={{4,0},{8,4},{12,8},{16,12},{20,16},{24,20},{28,24},{5,1},{9,5},{13... | collective-permute-start | bytes 6291464 | tf_op jit(solution)/shard_map/ppermute | solution.py:19
  16.6 99.1 %copy-start = (f32[32,2,128,128]{3,2,1,0:T(8,128)S(1)}, f32[32,2,128,128]{3,2,1,0:T(8,128)}, u32[]{:S(2)}) copy-start(f32[32,2,128,128]{3,2,1,0:T(8,128)} %param.5) | copy-start | bytes 12582916
  16.6 96.5 %collective-permute-start = (f32[3,1,128,128]{3,2,1,0:T(8,128)S(1)}, f32[3,1,128,128]{3,2,1,0:T(8,128)S(1)}, u32[]{:S(2)}, u32[]{:S(2)}) collective-permute-start(f32[3,1,128,128]{3,2,1,0:T(8,128)S(1)} %get-tuple-element.19), channel_id=1, source_target_pairs={{0,4},{4,8},{8,12},{12,16},{16,20},{20,24},{24,28},{1,5},{5,9},{9,... | collective-permute-start | bytes 589832 | tf_op jit(solution)/shard_map/ppermute | solution.py:16
  21.5 91.7 %collective-permute-start.1 = (f32[3,1,128,128]{3,2,1,0:T(8,128)S(1)}, f32[3,1,128,128]{3,2,1,0:T(8,128)S(1)}, u32[]{:S(2)}, u32[]{:S(2)}) collective-permute-start(f32[3,1,128,128]{3,2,1,0:T(8,128)S(1)} %get-tuple-element.20), channel_id=1, source_target_pairs={{4,0},{8,4},{12,8},{16,12},{20,16},{24,20},{28,24},{5,1},{9,5},{13... | collective-permute-start | bytes 589832 | tf_op jit(solution)/shard_map/ppermute | solution.py:19
  115.7 14.1 %copy-start.4 = (f32[32,1,128,128]{3,2,1,0:T(8,128)}, f32[32,1,128,128]{3,2,1,0:T(8,128)S(1)}, u32[]{:S(2)}) copy-start(f32[32,1,128,128]{3,2,1,0:T(8,128)S(1)} %collective-permute-done.2) | copy-start | bytes 6291460
  115.7 14.1 %copy-start.5 = (f32[32,1,128,128]{3,2,1,0:T(8,128)}, f32[32,1,128,128]{3,2,1,0:T(8,128)S(1)}, u32[]{:S(2)}) copy-start(f32[32,1,128,128]{3,2,1,0:T(8,128)S(1)} %collective-permute-done.3) | copy-start | bytes 6291460
  146.3 96.0 %copy-start.1 = (f32[32,2,128,128]{3,2,1,0:T(8,128)S(1)}, f32[32,2,128,128]{3,2,1,0:T(8,128)}, u32[]{:S(2)}) copy-start(f32[32,2,128,128]{3,2,1,0:T(8,128)} %fusion.29) | copy-start | bytes 12582916
  148.9 93.3 %collective-permute-start.5 = (f32[32,1,128,128]{3,2,1,0:T(8,128)S(1)}, f32[32,1,128,128]{3,2,1,0:T(8,128)S(1)}, u32[]{:S(2)}, u32[]{:S(2)}) collective-permute-start(f32[32,1,128,128]{3,2,1,0:T(8,128)S(1)} %get-tuple-element.10), channel_id=1, source_target_pairs={{0,4},{4,8},{8,12},{12,16},{16,20},{20,24},{24,28},{1,5},{5,9},{9,... | collective-permute-start | bytes 6291464 | tf_op jit(solution)/shard_map/ppermute | solution.py:16
  153.4 88.8 %collective-permute-start.4 = (f32[32,1,128,128]{3,2,1,0:T(8,128)S(1)}, f32[32,1,128,128]{3,2,1,0:T(8,128)S(1)}, u32[]{:S(2)}, u32[]{:S(2)}) collective-permute-start(f32[32,1,128,128]{3,2,1,0:T(8,128)S(1)} %get-tuple-element.11), channel_id=1, source_target_pairs={{4,0},{8,4},{12,8},{16,12},{20,16},{24,20},{28,24},{5,1},{9,5},{13... | collective-permute-start | bytes 6291464 | tf_op jit(solution)/shard_map/ppermute | solution.py:19
  156.1 93.7 %copy-start.7 = (f32[2,128,128]{2,1,0:T(8,128)S(1)}, f32[2,128,128]{2,1,0:T(8,128)}, u32[]{:S(2)}) copy-start(f32[2,128,128]{2,1,0:T(8,128)} %get-tuple-element.27) | copy-start | bytes 393220
  156.1 93.7 %copy-start.8 = (f32[2,128,128]{2,1,0:T(8,128)S(1)}, f32[2,128,128]{2,1,0:T(8,128)}, u32[]{:S(2)}) copy-start(f32[2,128,128]{2,1,0:T(8,128)} %get-tuple-element.34) | copy-start | bytes 393220
  156.1 93.7 %copy-start.9 = (f32[2,128,128]{2,1,0:T(8,128)S(1)}, f32[2,128,128]{2,1,0:T(8,128)}, u32[]{:S(2)}) copy-start(f32[2,128,128]{2,1,0:T(8,128)} %get-tuple-element.36) | copy-start | bytes 393220
  156.1 93.7 %copy-start.10 = (f32[2,128,128]{2,1,0:T(8,128)S(1)}, f32[2,128,128]{2,1,0:T(8,128)}, u32[]{:S(2)}) copy-start(f32[2,128,128]{2,1,0:T(8,128)} %param.9) | copy-start | bytes 393220
  242.2 7.6 %copy-start.2 = (f32[32,1,128,128]{3,2,1,0:T(8,128)}, f32[32,1,128,128]{3,2,1,0:T(8,128)S(1)}, u32[]{:S(2)}) copy-start(f32[32,1,128,128]{3,2,1,0:T(8,128)S(1)} %collective-permute-done.5) | copy-start | bytes 6291460
  242.2 7.6 %copy-start.3 = (f32[32,1,128,128]{3,2,1,0:T(8,128)}, f32[32,1,128,128]{3,2,1,0:T(8,128)S(1)}, u32[]{:S(2)}) copy-start(f32[32,1,128,128]{3,2,1,0:T(8,128)S(1)} %collective-permute-done.4) | copy-start | bytes 6291460
Sparse Core Ops, SparseCore 0:
  333.2 120.6 all-reduce.4
where the time goes:
time: 496 us; the launch traced here: 494 us
  waiting for transfers between devices  297 us (60%)
  other arithmetic  75.5 us (15%)
  blocking collectives  50.8 us (10%)
  local copies, waits for them, and re-layouts  25 us (5%)
  starting transfers between devices  18.4 us (4%)
  between operations  14.3 us (3%)
  matrix products  13 us (3%)
    ppermute x3, waiting for transfers between devices, extended(): lax.ppermute(lax.slice_in_dim(block, block.shape[dim] - width, None, axis...  176 us
    psum x1, waiting for transfers between devices, per_device(): low_factor = jnp.linalg.cholesky(lax.psum(gram_local, ('space', 'probe')))  121 us
    all_to_all x1, blocking collectives, per_device(): lax.all_to_all(hess_full, 'probe', split_axis=2, concat_axis=0, tiled=True)  50.8 us
    concatenate x3, other arithmetic, extended(): block = jnp.concatenate([low, block, high], axis=dim)  22.1 us
    mul x1, other arithmetic, per_device(): weighted = obs_weight * stencil(values_pad, wind_pad, False)  16.5 us
    ppermute x3, starting transfers between devices, extended(): lax.ppermute(lax.slice_in_dim(block, block.shape[dim] - width, None, axis...  14.3 us
    another operation x3, other arithmetic, per_device(): low_factor = jnp.linalg.cholesky(lax.psum(gram_local, ('space', 'probe')))  12.4 us
    add x1, other arithmetic, per_device(): hess_full = stencil(weighted_pad, wind_pad, True) + prior_weight * probes  10.8 us
  transfers between devices with their start and end apart: 7, of which 3 were waited for; matrix products, arithmetic and copies ran while one was open for 1% of the time, Pallas kernels for 0%

commit v1 on v0

v1 whole, which is shorter than its diff:
```python
import functools
import math

import jax
import jax.numpy as jnp
from jax import lax
from jax.experimental import pallas as pl
from jax.experimental.pallas import tpu as pltpu
from jax.sharding import PartitionSpec as P

diffusion = 0.1
MESH = pl.DeviceIdType.MESH
highest = lax.Precision.HIGHEST


def select_wind(winds, wind_step):
    levels = jnp.arange(winds.shape[0], dtype=jnp.int32)
    picked = levels[:, None] == wind_step[None, :]
    return jnp.sum(jnp.where(picked[:, None, :, None, None], winds, jnp.zeros_like(winds)), axis=0)


def exchange_kernel(
    n_space, n_probe, chunks, window,
    probes_ref, fields_ref, y_out, gram_out,
    field, fwd_state, coef, weighted, image, rows_ref, gram_part, reduce_buf, group_buf, total,
    own_sem, x_send, x_recv, zd_send, zf_send, lo_recv, hi_recv,
    f_own, f_xs, f_xr, f_zds, f_zfs, f_lor, f_hir,
    a_send, a_recv, a_own, r_send, r_recv, g_send, g_recv, t_send, t_recv, y_sem,
):
    space = lax.axis_index("space")
    probe = lax.axis_index("probe")
    side = lax.rem(space, 2)
    partner = space + 1 - 2 * side
    group = lax.div(space, 2)
    n_group = n_space // 2
    base = space - side
    n_peer = 2 * n_probe
    mine = side * n_probe + probe
    half = probes_ref.shape[0] // 2
    per = half // chunks
    ny, nz = probes_ref.shape[2], probes_ref.shape[3]
    band = ny // n_probe
    below, above = space - 2, space + 2
    has_lo, has_hi = group > 0, group < n_group - 1

    def peer(step):
        other = lax.rem(mine + step, n_peer)
        return other, lax.div(other, n_probe), lax.rem(other, n_probe)

    def sister(step):
        other = lax.rem(group + step, n_group)
        return other, 2 * other + side

    barrier = pltpu.get_barrier_semaphore()
    for step in range(1, n_peer):
        _, px, pp = peer(step)
        pl.semaphore_signal(barrier, inc=1, device_id=(base + px, pp), device_id_type=MESH)
    for step in range(1, n_group):
        pl.semaphore_signal(
            barrier, inc=1, device_id=(sister(step)[1], probe), device_id_type=MESH
        )
    pl.semaphore_wait(barrier, n_peer + n_group - 2)

    def remote(src, dst, send, recv, dev):
        return pltpu.make_async_remote_copy(
            src_ref=src, dst_ref=dst, send_sem=send, recv_sem=recv,
            device_id=dev, device_id_type=MESH,
        )

    own_plane = 2 + 2 * side
    got_plane = 4 - 2 * side

    own_f = pltpu.make_async_copy(fields_ref, field.at[pl.ds(1 + 2 * side, 2)], f_own)
    own_f.start()
    x_f = remote(fields_ref, field.at[pl.ds(1 + 2 * side, 2)], f_xs, f_xr, (partner, probe))
    x_f.start()

    def z_low(src, send):
        return remote(src, field.at[5, pl.ds(0, 4)], send, f_hir, (below, probe))

    def z_high(src, send):
        return remote(src, field.at[0, pl.ds(0, 4)], send, f_lor, (above, probe))

    direct_lo = (side == 0) & has_lo
    direct_hi = (side == 1) & has_hi
    relay_hi = (side == 0) & has_hi
    relay_lo = (side == 1) & has_lo

    @pl.when(direct_lo)
    def _():
        z_low(fields_ref.at[0, pl.ds(0, 4)], f_zds).start()

    @pl.when(direct_hi)
    def _():
        z_high(fields_ref.at[1, pl.ds(0, 4)], f_zds).start()

    def chunk_at(c):
        return pl.ds(c * per, per)

    def x_copy(c):
        return remote(
            probes_ref.at[pl.ds((1 - side) * half + c * per, per)],
            fwd_state.at[chunk_at(c), pl.ds(own_plane, 2)],
            x_send.at[c], x_recv.at[c], (partner, probe),
        )

    def own_copy(c):
        return pltpu.make_async_copy(
            probes_ref.at[pl.ds(side * half + c * per, per)],
            fwd_state.at[chunk_at(c), pl.ds(own_plane, 2)],
            own_sem.at[c],
        )

    def zd_src(c):
        return probes_ref.at[pl.ds(side * half + c * per, per)]

    def zf_src(c):
        return fwd_state.at[chunk_at(c), pl.ds(got_plane, 2)]

    def lo_copy(src, c, send):
        return remote(
            src, fwd_state.at[chunk_at(c), pl.ds(6, 2)], send.at[c], hi_recv.at[c], (below, probe)
        )

    def hi_copy(src, c, send):
        return remote(
            src, fwd_state.at[chunk_at(c), pl.ds(0, 2)], send.at[c], lo_recv.at[c], (above, probe)
        )

    def launch(c):
        x_copy(c).start()
        own_copy(c).start()

        @pl.when(direct_lo)
        def _():
            lo_copy(zd_src(c), c, zd_send).start()

        @pl.when(direct_hi)
        def _():
            hi_copy(zd_src(c), c, zd_send).start()

    for c in range(window):
        launch(c)

    @pl.when(jnp.logical_not(has_lo))
    def _():
        field[0] = jnp.zeros(field.shape[1:], jnp.float32)

        def clear(i, carry):
            fwd_state[i, pl.ds(0, 2)] = jnp.zeros((2, ny, nz), jnp.float32)
            return carry

        lax.fori_loop(0, half, clear, 0)

    @pl.when(jnp.logical_not(has_hi))
    def _():
        field[5] = jnp.zeros(field.shape[1:], jnp.float32)

        def clear(i, carry):
            fwd_state[i, pl.ds(6, 2)] = jnp.zeros((2, ny, nz), jnp.float32)
            return carry

        lax.fori_loop(0, half, clear, 0)

    x_f.wait_recv()

    @pl.when(relay_hi)
    def _():
        z_high(field.at[4, pl.ds(0, 4)], f_zfs).start()

    @pl.when(relay_lo)
    def _():
        z_low(field.at[1, pl.ds(0, 4)], f_zfs).start()

    own_f.wait()

    @pl.when(has_lo)
    def _():
        z_high(field.at[0, pl.ds(0, 4)], f_zfs).wait_recv()

    @pl.when(has_hi)
    def _():
        z_low(field.at[5, pl.ds(0, 4)], f_zfs).wait_recv()

    row_id = lax.broadcasted_iota(jnp.int32, (ny, nz), 0)
    col_id = lax.broadcasted_iota(jnp.int32, (ny, nz), 1)

    def make_coef(plane, carry):
        centre = jnp.full((ny, nz), 1.0 - 6.0 * diffusion, jnp.float32)
        for dim in range(3):
            speed = field[plane, dim]
            pos, neg = jnp.maximum(speed, 0.0), jnp.minimum(speed, 0.0)
            centre = centre - pos + neg
            up, down = pos + diffusion, diffusion - neg
            if dim == 1:
                up = jnp.where(row_id == 0, 0.0, up)
                down = jnp.where(row_id == ny - 1, 0.0, down)
            if dim == 2:
                up = jnp.where(col_id == 0, 0.0, up)
                down = jnp.where(col_id == nz - 1, 0.0, down)
            coef[plane, 1 + 2 * dim] = up
            coef[plane, 2 + 2 * dim] = down
        coef[plane, 0] = centre
        return carry

    lax.fori_loop(0, 6, make_coef, 0)

    def one_probe(i, carry):
        def tangent(plane, inner):
            u = fwd_state[i, plane + 1]
            out = coef[plane, 0] * u
            out += coef[plane, 1] * fwd_state[i, plane]
            out += coef[plane, 2] * fwd_state[i, plane + 2]
            out += coef[plane, 3] * pltpu.roll(u, 1, 0)
            out += coef[plane, 4] * pltpu.roll(u, ny - 1, 0)
            out += coef[plane, 5] * pltpu.roll(u, 1, 1)
            out += coef[plane, 6] * pltpu.roll(u, nz - 1, 1)
            weighted[plane] = field[plane, 3] * out
            return inner

        lax.fori_loop(0, 6, tangent, 0)

        def adjoint(at, inner):
            plane = at + 1
            v = weighted[plane]
            out = coef[plane, 0] * v + field[plane, 4] * fwd_state[i, plane + 1]
            out += coef[plane + 1, 1] * weighted[plane + 1]
            out += coef[plane - 1, 2] * weighted[plane - 1]
            out += pltpu.roll(coef[plane, 3] * v, ny - 1, 0)
            out += pltpu.roll(coef[plane, 4] * v, 1, 0)
            out += pltpu.roll(coef[plane, 5] * v, nz - 1, 1)
            out += pltpu.roll(coef[plane, 6] * v, 1, 1)
            image[i, at] = out
            return inner

        lax.fori_loop(0, 4, adjoint, 0)
        return carry

    def block_src(first, count, px, pp):
        return image.at[pl.ds(first, count), pl.ds(2 * px, 2), pl.ds(pp * band, band)]

    def block_dst(owner, first, count):
        return rows_ref.at[pl.ds(owner * half + first, count)]

    def rank_of(px, pp):
        return pp * 2 + px

    my_rank = rank_of(side, probe)

    def step_body(c, carry):
        @pl.when(c < chunks)
        def _():
            x_copy(c).wait_recv()

            @pl.when(relay_hi)
            def _():
                hi_copy(zf_src(c), c, zf_send).start()

            @pl.when(relay_lo)
            def _():
                lo_copy(zf_src(c), c, zf_send).start()

            @pl.when(c + window < chunks)
            def _():
                launch(c + window)

        @pl.when(c > 0)
        def _():
            d = c - 1
            own_copy(d).wait()

            @pl.when(has_lo)
            def _():
                hi_copy(zf_src(d), d, zf_send).wait_recv()

            @pl.when(has_hi)
            def _():
                lo_copy(zf_src(d), d, zf_send).wait_recv()

            lax.fori_loop(d * per, (d + 1) * per, one_probe, 0)
            for step in range(1, n_peer):
                _, px, pp = peer(step)
                remote(
                    block_src(d * per, per, px, pp), block_dst(my_rank, d * per, per),
                    a_send.at[step], a_recv.at[n_peer - step], (base + px, pp),
                ).start()
            pltpu.make_async_copy(
                block_src(d * per, per, side, probe), block_dst(my_rank, d * per, per), a_own
            ).start()

        return carry

    lax.fori_loop(0, chunks + 1, step_body, 0)

    for step in range(1, n_peer):
        _, px, pp = peer(step)
        remote(
            block_src(0, half, px, pp), block_dst(rank_of(px, pp), 0, half),
            a_send.at[step], a_recv.at[step], (base + px, pp),
        ).wait()
    pltpu.make_async_copy(
        block_src(0, half, side, probe), block_dst(my_rank, 0, half), a_own
    ).wait()

    y_copy = pltpu.make_async_copy(rows_ref, y_out, y_sem)
    y_copy.start()

    count = rows_ref.shape[0]
    depth = rows_ref.shape[1] * band
    flat = rows_ref.reshape(count * depth, nz)
    gram_part[...] = jnp.zeros_like(gram_part)

    def gram_step(t, carry):
        cols = jnp.concatenate(
            [flat[pl.ds(t * 8 + r, count, stride=depth), :] for r in range(8)], axis=1
        )
        gram_part[...] += lax.dot_general(
            cols, cols, (((1,), (1,)), ((), ())), precision=highest,
            preferred_element_type=jnp.float32,
        )
        return carry

    lax.fori_loop(0, depth // 8, gram_step, 0)

    share = count // n_peer

    def r_copy(step):
        other, px, pp = peer(step)
        return remote(
            gram_part.at[pl.ds(other * share, share)], reduce_buf.at[mine],
            r_send.at[step], r_recv.at[n_peer - step], (base + px, pp),
        )

    for step in range(1, n_peer):
        r_copy(step).start()
    reduce_buf[mine] = gram_part[pl.ds(pl.multiple_of(mine * share, share), share)]
    for step in range(1, n_peer):
        r_copy(step).wait_recv()
    group_buf[group] = jnp.sum(reduce_buf[...], axis=0)

    def g_copy(step):
        other, at = sister(step)
        return remote(
            group_buf.at[group], group_buf.at[group],
            g_send.at[step], g_recv.at[n_group - step], (at, probe),
        )

    for step in range(1, n_group):
        g_copy(step).start()
    for step in range(1, n_group):
        g_copy(step).wait_recv()
    total[pl.ds(pl.multiple_of(mine * share, share), share)] = jnp.sum(group_buf[...], axis=0)

    def t_copy(step):
        _, px, pp = peer(step)
        return remote(
            total.at[pl.ds(mine * share, share)], total.at[pl.ds(mine * share, share)],
            t_send.at[step], t_recv.at[n_peer - step], (base + px, pp),
        )

    for step in range(1, n_peer):
        t_copy(step).start()
    for step in range(1, n_peer):
        t_copy(step).wait_recv()
    gram_out[...] = total[...]

    for step in range(1, n_peer):
        r_copy(step).wait_send()
        t_copy(step).wait_send()
    for step in range(1, n_group):
        g_copy(step).wait_send()
    x_f.wait_send()

    @pl.when(direct_lo)
    def _():
        z_low(fields_ref.at[0, pl.ds(0, 4)], f_zds).wait_send()

    @pl.when(direct_hi)
    def _():
        z_high(fields_ref.at[1, pl.ds(0, 4)], f_zds).wait_send()

    @pl.when(relay_hi)
    def _():
        z_high(field.at[4, pl.ds(0, 4)], f_zfs).wait_send()

    @pl.when(relay_lo)
    def _():
        z_low(field.at[1, pl.ds(0, 4)], f_zfs).wait_send()

    def drain(c, carry):
        x_copy(c).wait_send()

        @pl.when(direct_lo)
        def _():
            lo_copy(zd_src(c), c, zd_send).wait_send()

        @pl.when(direct_hi)
        def _():
            hi_copy(zd_src(c), c, zd_send).wait_send()

        @pl.when(relay_hi)
        def _():
            hi_copy(zf_src(c), c, zf_send).wait_send()

        @pl.when(relay_lo)
        def _():
            lo_copy(zf_src(c), c, zf_send).wait_send()

        return carry

    lax.fori_loop(0, chunks, drain, 0)
    y_copy.wait()


def exchange(probes, fields, n_space, n_probe, chunks=8, window=2):
    local, planes, ny, nz = probes.shape
    count = local * n_probe
    half = local // 2
    band = ny // n_probe
    n_peer, n_group = 2 * n_probe, n_space // 2
    share = count // n_peer
    f32 = jnp.float32
    dma = pltpu.SemaphoreType.DMA
    return pl.pallas_call(
        functools.partial(exchange_kernel, n_space, n_probe, chunks, window),
        out_shape=(
            jax.ShapeDtypeStruct((count, planes, band, nz), f32),
            jax.ShapeDtypeStruct((count, count), f32),
        ),
        in_specs=[pl.BlockSpec(memory_space=pl.ANY)] * 2,
        out_specs=(
            pl.BlockSpec(memory_space=pl.ANY),
            pl.BlockSpec(memory_space=pltpu.VMEM),
        ),
        scratch_shapes=[
            pltpu.VMEM((6, 5, ny, nz), f32),
            pltpu.VMEM((half, 8, ny, nz), f32),
            pltpu.VMEM((6, 7, ny, nz), f32),
            pltpu.VMEM((6, ny, nz), f32),
            pltpu.VMEM((half, 4, ny, nz), f32),
            pltpu.VMEM((count, planes, band, nz), f32),
            pltpu.VMEM((count, count), f32),
            pltpu.VMEM((n_peer, share, count), f32),
            pltpu.VMEM((n_group, share, count), f32),
            pltpu.VMEM((count, count), f32),
        ]
        + [dma((chunks,))] * 7
        + [dma(())] * 7
        + [dma((n_peer,)), dma((n_peer,)), dma(())]
        + [dma((n_peer,)), dma((n_peer,)), dma((n_group,)), dma((n_group,))]
        + [dma((n_peer,)), dma((n_peer,)), dma(())],
        compiler_params=pltpu.CompilerParams(
            collective_id=0, has_side_effects=True, vmem_limit_bytes=48 * 1024 * 1024
        ),
        name="exchange",
    )(probes, fields)


def basis_kernel(inverse_ref, y_ref, out_ref):
    count, rows, nz = y_ref.shape
    flat = y_ref.reshape(count * rows, nz)
    result_flat = out_ref.reshape(count * rows, nz)
    cols = jnp.concatenate(
        [flat[pl.ds(r, count, stride=rows), :] for r in range(rows)], axis=1
    )
    result = jnp.dot(
        inverse_ref[...], cols, precision=highest, preferred_element_type=jnp.float32
    )
    for r in range(rows):
        result_flat[pl.ds(r, count, stride=rows), :] = result[:, r * nz : (r + 1) * nz]


def basis(inverse, y_rows, rows=8):
    count, depth, nz = y_rows.shape
    block = pl.BlockSpec((count, rows, nz), lambda i: (0, i, 0))
    return pl.pallas_call(
        basis_kernel,
        grid=(depth // rows,),
        out_shape=jax.ShapeDtypeStruct(y_rows.shape, jnp.float32),
        in_specs=[pl.BlockSpec((count, count), lambda i: (0, 0)), block],
        out_specs=block,
        compiler_params=pltpu.CompilerParams(vmem_limit_bytes=32 * 1024 * 1024),
        name="basis",
    )(inverse, y_rows)


def per_device(probes, winds, wind_step, obs_weight, prior_weight):
    n_space, n_probe = lax.axis_size("space"), lax.axis_size("probe")
    wind_now = select_wind(winds, wind_step)
    fields = jnp.concatenate([wind_now, obs_weight[None], prior_weight[None]], axis=0)
    fields = jnp.swapaxes(fields, 0, 1)
    image, gram_matrix = exchange(probes, fields, n_space, n_probe)
    low_factor = jnp.linalg.cholesky(gram_matrix)
    cells_all = image[0].size * n_space * n_probe
    norm_scale = math.sqrt(cells_all)
    eye = jnp.eye(low_factor.shape[0], dtype=jnp.float32)
    inverse = jax.scipy.linalg.solve_triangular(low_factor, eye, lower=True) * norm_scale
    count, planes, band, nz = image.shape
    basis_out = basis(inverse, image.reshape(count, planes * band, nz)).reshape(image.shape)
    return (basis_out, low_factor.T / norm_scale)


def solution(mesh):
    placed = (
        P("probe", "space", None, None),
        P(None, None, "space", None, None),
        P("space"),
        P("space", None, None),
        P("space", None, None),
    )
    return jax.shard_map(
        per_device,
        mesh=mesh,
        in_specs=placed,
        out_specs=(P(None, "space", "probe", None), P()),
        check_vma=False,
    )
```

time: 496 us -> 167 us (0.34)
  waiting for transfers between devices: 297 us -> 0 us
  Pallas kernels: 0 us -> 135 us
  blocking collectives: 50.8 us -> 0 us
  other arithmetic: 75.5 us -> 25.3 us
  local copies, waits for them, and re-layouts: 25 us -> 5.02 us
  starting transfers between devices: 18.4 us -> 0 us
  between operations: 14.3 us -> 0.74 us
  matrix products: 13 us -> 0.25 us
    ppermute x6 -> x0, waiting for transfers between devices: 176 us -> none  [the longest x3 176 us: extended(): lax.ppermute(lax.slice_in_dim(block, block.shape[dim] - width, None, axis...]
    pallas_call x0 -> x2, Pallas kernels: none -> 135 us  [the longest x1 129 us: exchange(): pl.pallas_call(functools.partial(exchange_kernel, n_space, n_probe, chunk...]
    psum x1 -> x0, waiting for transfers between devices: 121 us -> none  [per_device(): low_factor = jnp.linalg.cholesky(lax.psum(gram_local, ('space', 'probe')))]
    all_to_all x1 -> x0, blocking collectives: 50.8 us -> none  [per_device(): lax.all_to_all(hess_full, 'probe', split_axis=2, concat_axis=0, tiled=True)]
    concatenate x3 -> x0, other arithmetic: 22.1 us -> none  [extended(): block = jnp.concatenate([low, block, high], axis=dim)]
    ppermute x6 -> x0, starting transfers between devices: 18.4 us -> none  [the longest x3 14.3 us: extended(): lax.ppermute(lax.slice_in_dim(block, block.shape[dim] - width, None, axis...]
    mul x1 -> x0, other arithmetic: 16.5 us -> none  [per_device(): weighted = obs_weight * stencil(values_pad, wind_pad, False)]
    add x1 -> x0, other arithmetic: 10.8 us -> none  [per_device(): hess_full = stencil(weighted_pad, wind_pad, True) + prior_weight * probes]
  transfers between devices with their start and end apart: 7 -> 0, of which waited for: 3 -> 0; matrix products, arithmetic and copies ran while one was open for 1% -> 0% of each run, Pallas kernels for 0% -> 0%
where the time goes in v1:
time: 167 us
  Pallas kernels  135 us (81%)
  other arithmetic  25.3 us (15%)
  local copies, waits for them, and re-layouts  5.02 us (3%)
    pallas_call x1, Pallas kernels, exchange(): pl.pallas_call(functools.partial(exchange_kernel, n_space, n_probe, chunk...  129 us
    another operation x3, other arithmetic, per_device(): low_factor = jnp.linalg.cholesky(gram_matrix)  12.4 us
    another operation x1, other arithmetic, per_device(): jax.scipy.linalg.solve_triangular(low_factor, eye, lower=True) * norm_scale  9.81 us
    pallas_call x1, Pallas kernels, basis(): pl.pallas_call(basis_kernel, grid=(depth // rows,), out_shape=jax.ShapeDt...  6.81 us
    unnamed x9, local copies, waits for them, and re-layouts  4.93 us

profile of v1, /device:TPU:0, one launch (start us, length us, event | category | flops | bytes accessed | tf_op | source)
XLA Modules:
  0.0 166.7 jit_solution(1461797632739217248)
XLA Ops:
  0.6 0.0 copy-start.2
  0.6 0.0 copy-start.3
  0.7 0.7 iota_compare_fusion.3
  1.4 1.6 select_reduce_fusion
  3.0 0.0 copy-done.2
  3.0 0.0 copy-done.3
  3.1 128.6 %exchange.1 = (f32[128,2,32,128]{3,2,1,0:T(8,128)S(1)}, f32[128,128]{1,0:T(8,128)S(1)}) custom-call(f32[32,2,128,128]{3,2,1,0:T(8,128)} %probes_ref.1, f32[2,5,128,128]{3,2,1,0:T(8,128)S(1)} %maximum_bitcast_fusion.fields_ref), custom_call_target="tpu_custom_call" | custom-call | tf_op jit(solution)/shard_map/exchange/pallas_call | solution.py:424
  131.7 0.0 copy-start
  131.7 2.0 %copy-done = f32[128,2,32,128]{3,2,1,0:T(8,128)} copy-done((f32[128,2,32,128]{3,2,1,0:T(8,128)}, f32[128,2,32,128]{3,2,1,0:T(8,128)S(1)}, u32[]{:S(2)}) %copy-start) | copy-done | bytes 4194328
  133.7 0.1 copy.10
  133.8 11.7 %cholesky.17 = f32[128,128]{1,0:T(8,128)S(1)} custom-call(f32[128,128]{1,0:T(8,128)S(1)} %fusion.1), custom_call_target="Cholesky" | custom-call | tf_op jit(solution)/shard_map/jit(cholesky)/cholesky | solution.py:493
  145.6 0.6 compare_reduce_fusion
  146.2 0.7 multiply_bitcast_fusion
  146.9 0.7 copy.11
  147.6 9.8 %custom-call.7 = f32[1,128,128]{1,2,0:T(8,128)S(1)} custom-call(f32[1,128,128]{2,1,0:T(8,128)S(1)} %get-tuple-element.11), custom_call_target="InvertDiagBlocksLowerTriangular" | custom-call | tf_op jit(solution)/shard_map/jit(_solve_triangular)/triangular_solve | solution.py:497
  157.4 0.3 convolution_multiply_fusion.inverse_ref
  157.7 0.0 copy-start.1
  157.7 2.2 %copy-done.1 = f32[128,2,32,128]{3,2,1,0:T(8,128)S(1)} copy-done((f32[128,2,32,128]{3,2,1,0:T(8,128)S(1)}, f32[128,2,32,128]{3,2,1,0:T(8,128)}, u32[]{:S(2)}) %copy-start.1) | copy-done | bytes 4194328
  159.9 6.8 %basis.1 = f32[128,64,128]{2,1,0:T(8,128)} custom-call(f32[128,128]{1,0:T(8,128)S(1)} %convolution_multiply_fusion.inverse_ref, f32[128,64,128]{2,1,0:T(8,128)S(1)} %bitcast.17), custom_call_target="tpu_custom_call" | custom-call | tf_op jit(solution)/shard_map/basis/pallas_call | solution.py:476
  (3 shorter events, 0.1 us)
Async XLA Ops:
  0.6 2.4 %copy-start.2 = (f32[2,128,128]{2,1,0:T(8,128)S(1)}, f32[2,128,128]{2,1,0:T(8,128)}, u32[]{:S(2)}) copy-start(f32[2,128,128]{2,1,0:T(8,128)} %param.9) | copy-start | bytes 393220
  0.6 2.4 %copy-start.3 = (f32[2,128,128]{2,1,0:T(8,128)S(1)}, f32[2,128,128]{2,1,0:T(8,128)}, u32[]{:S(2)}) copy-start(f32[2,128,128]{2,1,0:T(8,128)} %param.8) | copy-start | bytes 393220
  131.7 2.0 %copy-start = (f32[128,2,32,128]{3,2,1,0:T(8,128)}, f32[128,2,32,128]{3,2,1,0:T(8,128)S(1)}, u32[]{:S(2)}) copy-start(f32[128,2,32,128]{3,2,1,0:T(8,128)S(1)} %get-tuple-element.5) | copy-start | bytes 12582916
  157.7 2.2 %copy-start.1 = (f32[128,2,32,128]{3,2,1,0:T(8,128)S(1)}, f32[128,2,32,128]{3,2,1,0:T(8,128)}, u32[]{:S(2)}) copy-start(f32[128,2,32,128]{3,2,1,0:T(8,128)} %copy-done) | copy-start | bytes 12582916

commit v2 on v1

--- a/solution.py
+++ b/solution.py
@@ -22,7 +22,7 @@
 def exchange_kernel(
     n_space, n_probe, chunks, window,
     probes_ref, fields_ref, y_out, gram_out,
-    field, fwd_state, coef, weighted, image, rows_ref, gram_part, reduce_buf, group_buf, total,
+    field, fwd_state, coef, weighted, image, rows_ref, gram_acc, gram_part, reduce_buf, group_buf, total,
     own_sem, x_send, x_recv, zd_send, zf_send, lo_recv, hi_recv,
     f_own, f_xs, f_xr, f_zds, f_zfs, f_lor, f_hir,
     a_send, a_recv, a_own, r_send, r_recv, g_send, g_recv, t_send, t_recv, y_sem,
@@ -308,19 +308,21 @@
     count = rows_ref.shape[0]
     depth = rows_ref.shape[1] * band
     flat = rows_ref.reshape(count * depth, nz)
-    gram_part[...] = jnp.zeros_like(gram_part)
+    gram_acc[...] = jnp.zeros_like(gram_acc)
 
     def gram_step(t, carry):
         cols = jnp.concatenate(
             [flat[pl.ds(t * 8 + r, count, stride=depth), :] for r in range(8)], axis=1
         )
-        gram_part[...] += lax.dot_general(
-            cols, cols, (((1,), (1,)), ((), ())), precision=highest,
-            preferred_element_type=jnp.float32,
+        both = jnp.concatenate(split(cols), axis=0)
+        gram_acc[...] += lax.dot_general(
+            both, both, (((1,), (1,)), ((), ())), preferred_element_type=jnp.float32
         )
         return carry
 
     lax.fori_loop(0, depth // 8, gram_step, 0)
+    across = gram_acc[:count, count:] + gram_acc[count:, :count]
+    gram_part[...] = gram_acc[:count, :count] + (across + gram_acc[count:, count:])
 
     share = count // n_peer
 
@@ -439,6 +441,7 @@
             pltpu.VMEM((6, ny, nz), f32),
             pltpu.VMEM((half, 4, ny, nz), f32),
             pltpu.VMEM((count, planes, band, nz), f32),
+            pltpu.VMEM((2 * count, 2 * count), f32),
             pltpu.VMEM((count, count), f32),
             pltpu.VMEM((n_peer, share, count), f32),
             pltpu.VMEM((n_group, share, count), f32),
@@ -456,32 +459,114 @@
     )(probes, fields)
 
 
-def basis_kernel(inverse_ref, y_ref, out_ref):
-    count, rows, nz = y_ref.shape
-    flat = y_ref.reshape(count * rows, nz)
-    result_flat = out_ref.reshape(count * rows, nz)
-    cols = jnp.concatenate(
-        [flat[pl.ds(r, count, stride=rows), :] for r in range(rows)], axis=1
-    )
-    result = jnp.dot(
-        inverse_ref[...], cols, precision=highest, preferred_element_type=jnp.float32
-    )
-    for r in range(rows):
-        result_flat[pl.ds(r, count, stride=rows), :] = result[:, r * nz : (r + 1) * nz]
-
-
-def basis(inverse, y_rows, rows=8):
+def split(values):
+    high = values.astype(jnp.bfloat16)
+    low = (values - high.astype(jnp.float32)).astype(jnp.bfloat16)
+    return high, low
+
+
+def factor(gram_ref, work, n, rows=8):
+    work[:, :n] = gram_ref[...]
+    row_id = lax.broadcasted_iota(jnp.int32, (n, n), 0)
+    col_id = lax.broadcasted_iota(jnp.int32, (n, n), 1)
+    work[:, n:] = jnp.where(row_id == col_id, 1.0, 0.0)
+    sub = lax.broadcasted_iota(jnp.int32, (rows, n), 0)
+    lane = lax.broadcasted_iota(jnp.int32, (rows, n), 1)
+
+    def panel_step(at, carry):
+        start = pl.multiple_of(at * rows, rows)
+        left = pltpu.roll(work[pl.ds(start, rows), :n], lax.rem(n - start, n), 1)
+        right = work[pl.ds(start, rows), n:]
+        for j in range(rows):
+            col = jnp.broadcast_to(left[:, j : j + 1], (rows, n))
+            pivot = jnp.broadcast_to(col[j : j + 1, :], (rows, n))
+            scale = lax.rsqrt(pivot)
+            scale = scale * (1.5 - 0.5 * (pivot * scale) * scale)
+            row_left = jnp.broadcast_to(left[j : j + 1, :], (rows, n)) * scale
+            row_right = jnp.broadcast_to(right[j : j + 1, :], (rows, n)) * scale
+            times = jnp.where(sub > j, col * scale, 0.0)
+            left = jnp.where(sub == j, row_left, left - times * row_left)
+            right = jnp.where(sub == j, row_right, right - times * row_right)
+        left = pltpu.roll(left, start, 1)
+        ahead = jnp.where(lane >= start + rows, left, 0.0)
+        both = jnp.concatenate([left, right], axis=1)
+        work[...] -= lax.dot_general(
+            ahead, both, (((0,), (0,)), ((), ())), precision=highest,
+            preferred_element_type=jnp.float32,
+        )
+        work[pl.ds(start, rows), :] = both
+        return carry
+
+    lax.fori_loop(0, n // rows, panel_step, 0)
+    upper = jnp.where(row_id <= col_id, work[:, :n], 0.0)
+    return upper, work[:, n:]
+
+
+def basis_kernel(
+    norm_scale, gram_ref, y_hbm, out_hbm, factor_ref, work, y_ref, out_ref, in_sem, out_sem
+):
+    count, depth, nz = y_ref.shape
+    fetch = pltpu.make_async_copy(y_hbm, y_ref, in_sem)
+    fetch.start()
+    upper, inverse = factor(gram_ref, work, count)
+    factor_ref[...] = upper / norm_scale
+    high, low = split(inverse * norm_scale)
+    left = jnp.concatenate([high, low, high, low], axis=1)
+    flat = y_ref.reshape(count * depth, nz)
+    result_flat = out_ref.reshape(count * depth, nz)
+    rows = 8
+    fetch.wait()
+
+    def store(t):
+        part = pl.ds(pl.multiple_of(t * rows, rows), rows)
+        return pltpu.make_async_copy(out_ref.at[:, part], out_hbm.at[:, part], out_sem.at[t])
+
+    def block_step(t, carry):
+        cols = jnp.concatenate(
+            [flat[pl.ds(t * rows + r, count, stride=depth), :] for r in range(rows)], axis=1
+        )
+        y_high, y_low = split(cols)
+        right = jnp.concatenate([y_high, y_high, y_low, y_low], axis=0)
+        result = jnp.dot(left, right, preferred_element_type=jnp.float32)
+        for r in range(rows):
+            result_flat[pl.ds(t * rows + r, count, stride=depth), :] = result[
+                :, r * nz : (r + 1) * nz
+            ]
+        store(t).start()
+        return carry
+
+    lax.fori_loop(0, depth // rows, block_step, 0)
+
+    def drain(t, carry):
+        store(t).wait()
+        return carry
+
+    lax.fori_loop(0, depth // rows, drain, 0)
+
+
+def basis(gram_matrix, y_rows, norm_scale):
     count, depth, nz = y_rows.shape
-    block = pl.BlockSpec((count, rows, nz), lambda i: (0, i, 0))
+    f32 = jnp.float32
+    vmem = pl.BlockSpec(memory_space=pltpu.VMEM)
+    hbm = pl.BlockSpec(memory_space=pl.ANY)
     return pl.pallas_call(
-        basis_kernel,
-        grid=(depth // rows,),
-        out_shape=jax.ShapeDtypeStruct(y_rows.shape, jnp.float32),
-        in_specs=[pl.BlockSpec((count, count), lambda i: (0, 0)), block],
-        out_specs=block,
-        compiler_params=pltpu.CompilerParams(vmem_limit_bytes=32 * 1024 * 1024),
+        functools.partial(basis_kernel, norm_scale),
+        out_shape=(
+            jax.ShapeDtypeStruct(y_rows.shape, f32),
+            jax.ShapeDtypeStruct(gram_matrix.shape, f32),
+        ),
+        in_specs=[vmem, hbm],
+        out_specs=(hbm, vmem),
+        scratch_shapes=[
+            pltpu.VMEM((count, 2 * count), f32),
+            pltpu.VMEM(y_rows.shape, f32),
+            pltpu.VMEM(y_rows.shape, f32),
+            pltpu.SemaphoreType.DMA(()),
+            pltpu.SemaphoreType.DMA((depth // 8,)),
+        ],
+        compiler_params=pltpu.CompilerParams(vmem_limit_bytes=56 * 1024 * 1024),
         name="basis",
-    )(inverse, y_rows)
+    )(gram_matrix, y_rows)
 
 
 def per_device(probes, winds, wind_step, obs_weight, prior_weight):
@@ -490,14 +575,12 @@
     fields = jnp.concatenate([wind_now, obs_weight[None], prior_weight[None]], axis=0)
     fields = jnp.swapaxes(fields, 0, 1)
     image, gram_matrix = exchange(probes, fields, n_space, n_probe)
-    low_factor = jnp.linalg.cholesky(gram_matrix)
-    cells_all = image[0].size * n_space * n_probe
-    norm_scale = math.sqrt(cells_all)
-    eye = jnp.eye(low_factor.shape[0], dtype=jnp.float32)
-    inverse = jax.scipy.linalg.solve_triangular(low_factor, eye, lower=True) * norm_scale
     count, planes, band, nz = image.shape
-    basis_out = basis(inverse, image.reshape(count, planes * band, nz)).reshape(image.shape)
-    return (basis_out, low_factor.T / norm_scale)
+    norm_scale = math.sqrt(planes * band * nz * n_space * n_probe)
+    basis_out, r_factor = basis(
+        gram_matrix, image.reshape(count, planes * band, nz), norm_scale
+    )
+    return (basis_out.reshape(image.shape), r_factor)
 
 
 def solution(mesh):

time: 167 us -> 163 us (0.976)
  other arithmetic: 25.3 us -> 2.4 us
  Pallas kernels: 135 us -> 157 us
  local copies, waits for them, and re-layouts: 5.02 us -> 2.55 us
    pallas_call x1, Pallas kernels: 6.81 us -> 29.6 us  [basis(): pl.pallas_call(functools.partial(basis_kernel, norm_scale), out_shape=(ja...]
    another operation x4 -> x0, other arithmetic: 22.2 us -> none  [the longest x3 12.4 us: per_device(): low_factor = jnp.linalg.cholesky(gram_matrix)]
    unnamed x9 -> x8, local copies, waits for them, and re-layouts: 4.93 us -> 2.55 us
where the time goes in v2:
time: 163 us; the launch traced here: 162 us
  Pallas kernels  157 us (96%)
  local copies, waits for them, and re-layouts  2.55 us (2%)
  other arithmetic  2.4 us (1%)
    pallas_call x1, Pallas kernels, exchange(): pl.pallas_call(functools.partial(exchange_kernel, n_space, n_probe, chunk...  127 us
    pallas_call x1, Pallas kernels, basis(): pl.pallas_call(functools.partial(basis_kernel, norm_scale), out_shape=(ja...  29.6 us

profile of v2, /device:TPU:0, one launch (start us, length us, event | category | flops | bytes accessed | tf_op | source)
XLA Modules:
  0.0 162.4 jit_solution(15154343645444191267)
XLA Ops:
  0.6 0.0 copy-start.2
  0.6 0.0 copy-start.3
  0.7 0.7 iota_compare_fusion
  1.4 1.6 %select_reduce_fusion = f32[3,2,128,128]{3,2,1,0:T(8,128)S(1)} fusion(f32[4,3,2,128,128]{4,3,2,1,0:T(8,128)} %param.6, pred[4,2]{1,0:T(4,128)(4,1)S(1)} %iota_compare_fusion), kind=kLoop, calls=%fused_computation | loop fusion | flops 688128 | bytes 1966088 | tf_op jit(solution)/shard_map/reduce_sum | solution.py:19
  3.0 0.0 copy-done.2
  3.0 0.0 copy-done.3
  3.1 127.2 %exchange.1 = (f32[128,2,32,128]{3,2,1,0:T(8,128)S(1)}, f32[128,128]{1,0:T(8,128)S(1)}) custom-call(f32[32,2,128,128]{3,2,1,0:T(8,128)} %probes_ref.1, f32[2,5,128,128]{3,2,1,0:T(8,128)S(1)} %maximum_bitcast_fusion.fields_ref), custom_call_target="tpu_custom_call" | custom-call | tf_op jit(solution)/shard_map/exchange/pallas_call | solution.py:426
  130.3 0.0 copy-start
  130.3 1.9 %copy-done = f32[128,2,32,128]{3,2,1,0:T(8,128)} copy-done((f32[128,2,32,128]{3,2,1,0:T(8,128)}, f32[128,2,32,128]{3,2,1,0:T(8,128)S(1)}, u32[]{:S(2)}) %copy-start) | copy-done | bytes 4194328
  132.2 0.0 copy-start.1
  132.2 0.6 copy-done.1
  132.8 29.6 %basis.1 = (f32[128,64,128]{2,1,0:T(8,128)}, f32[128,128]{1,0:T(8,128)}) custom-call(f32[128,128]{1,0:T(8,128)} %copy-done.1, f32[128,64,128]{2,1,0:T(8,128)} %bitcast.6), custom_call_target="tpu_custom_call" | custom-call | tf_op jit(solution)/shard_map/basis/pallas_call | solution.py:552
  (1 shorter events, 0.0 us)
Async XLA Ops:
  0.6 2.4 %copy-start.2 = (f32[2,128,128]{2,1,0:T(8,128)S(1)}, f32[2,128,128]{2,1,0:T(8,128)}, u32[]{:S(2)}) copy-start(f32[2,128,128]{2,1,0:T(8,128)} %param.9) | copy-start | bytes 393220
  0.6 2.4 %copy-start.3 = (f32[2,128,128]{2,1,0:T(8,128)S(1)}, f32[2,128,128]{2,1,0:T(8,128)}, u32[]{:S(2)}) copy-start(f32[2,128,128]{2,1,0:T(8,128)} %param.8) | copy-start | bytes 393220
  130.3 1.9 %copy-start = (f32[128,2,32,128]{3,2,1,0:T(8,128)}, f32[128,2,32,128]{3,2,1,0:T(8,128)S(1)}, u32[]{:S(2)}) copy-start(f32[128,2,32,128]{3,2,1,0:T(8,128)S(1)} %get-tuple-element.7) | copy-start | bytes 12582916
  132.2 0.6 copy-start.1

commit v3 on v2

--- a/solution.py
+++ b/solution.py
@@ -24,7 +24,7 @@
     probes_ref, fields_ref, y_out, gram_out,
     field, fwd_state, coef, weighted, image, rows_ref, gram_acc, gram_part, reduce_buf, group_buf, total,
     own_sem, x_send, x_recv, zd_send, zf_send, lo_recv, hi_recv,
-    f_own, f_xs, f_xr, f_zds, f_zfs, f_lor, f_hir,
+    f_own, f_xs, f_xr, f_zds, f_zfs, f_lor, f_hir, s_send, s_recv,
     a_send, a_recv, a_own, r_send, r_recv, g_send, g_recv, t_send, t_recv, y_sem,
 ):
     space = lax.axis_index("space")
@@ -70,16 +70,48 @@
     own_plane = 2 + 2 * side
     got_plane = 4 - 2 * side
 
+    band_at = pl.ds(probe * band, band)
     own_f = pltpu.make_async_copy(fields_ref, field.at[pl.ds(1 + 2 * side, 2)], f_own)
     own_f.start()
-    x_f = remote(fields_ref, field.at[pl.ds(1 + 2 * side, 2)], f_xs, f_xr, (partner, probe))
+    x_f = remote(
+        fields_ref.at[:, :, band_at], field.at[pl.ds(1 + 2 * side, 2), :, band_at],
+        f_xs, f_xr, (partner, probe),
+    )
     x_f.start()
 
-    def z_low(src, send):
-        return remote(src, field.at[5, pl.ds(0, 4)], send, f_hir, (below, probe))
-
-    def z_high(src, send):
-        return remote(src, field.at[0, pl.ds(0, 4)], send, f_lor, (above, probe))
+    def z_low(src, plane, send):
+        return remote(
+            src.at[plane, pl.ds(0, 4), band_at], field.at[5, pl.ds(0, 4), band_at],
+            send, f_hir, (below, probe),
+        )
+
+    def z_high(src, plane, send):
+        return remote(
+            src.at[plane, pl.ds(0, 4), band_at], field.at[0, pl.ds(0, 4), band_at],
+            send, f_lor, (above, probe),
+        )
+
+    def share_copy(kind, step):
+        if kind == 0:
+            ref = field.at[pl.ds(3 - 2 * side, 2), :, band_at]
+        else:
+            ref = field.at[0 if kind == 1 else 5, pl.ds(0, 4), band_at]
+        to = lax.rem(probe + step, n_probe)
+        return remote(
+            ref, ref, s_send.at[kind, step], s_recv.at[kind, n_probe - step], (space, to)
+        )
+
+    def share_start(kind):
+        for step in range(1, n_probe):
+            share_copy(kind, step).start()
+
+    def share_wait(kind):
+        for step in range(1, n_probe):
+            share_copy(kind, step).wait_recv()
+
+    def share_drain(kind):
+        for step in range(1, n_probe):
+            share_copy(kind, step).wait_send()
 
     direct_lo = (side == 0) & has_lo
     direct_hi = (side == 1) & has_hi
@@ -88,11 +120,11 @@
 
     @pl.when(direct_lo)
     def _():
-        z_low(fields_ref.at[0, pl.ds(0, 4)], f_zds).start()
+        z_low(fields_ref, 0, f_zds).start()
 
     @pl.when(direct_hi)
     def _():
-        z_high(fields_ref.at[1, pl.ds(0, 4)], f_zds).start()
+        z_high(fields_ref, 1, f_zds).start()
 
     def chunk_at(c):
         return pl.ds(c * per, per)
@@ -166,21 +198,34 @@
 
     @pl.when(relay_hi)
     def _():
-        z_high(field.at[4, pl.ds(0, 4)], f_zfs).start()
+        z_high(field, 4, f_zfs).start()
 
     @pl.when(relay_lo)
     def _():
-        z_low(field.at[1, pl.ds(0, 4)], f_zfs).start()
+        z_low(field, 1, f_zfs).start()
+
+    share_start(0)
+
+    @pl.when(has_lo)
+    def _():
+        z_high(field, 0, f_zfs).wait_recv()
+        share_start(1)
+
+    @pl.when(has_hi)
+    def _():
+        z_low(field, 5, f_zfs).wait_recv()
+        share_start(2)
 
     own_f.wait()
+    share_wait(0)
 
     @pl.when(has_lo)
     def _():
-        z_high(field.at[0, pl.ds(0, 4)], f_zfs).wait_recv()
+        share_wait(1)
 
     @pl.when(has_hi)
     def _():
-        z_low(field.at[5, pl.ds(0, 4)], f_zfs).wait_recv()
+        share_wait(2)
 
     row_id = lax.broadcasted_iota(jnp.int32, (ny, nz), 0)
     col_id = lax.broadcasted_iota(jnp.int32, (ny, nz), 1)
@@ -372,22 +417,31 @@
     for step in range(1, n_group):
         g_copy(step).wait_send()
     x_f.wait_send()
+    share_drain(0)
+
+    @pl.when(has_lo)
+    def _():
+        share_drain(1)
+
+    @pl.when(has_hi)
+    def _():
+        share_drain(2)
 
     @pl.when(direct_lo)
     def _():
-        z_low(fields_ref.at[0, pl.ds(0, 4)], f_zds).wait_send()
+        z_low(fields_ref, 0, f_zds).wait_send()
 
     @pl.when(direct_hi)
     def _():
-        z_high(fields_ref.at[1, pl.ds(0, 4)], f_zds).wait_send()
+        z_high(fields_ref, 1, f_zds).wait_send()
 
     @pl.when(relay_hi)
     def _():
-        z_high(field.at[4, pl.ds(0, 4)], f_zfs).wait_send()
+        z_high(field, 4, f_zfs).wait_send()
 
     @pl.when(relay_lo)
     def _():
-        z_low(field.at[1, pl.ds(0, 4)], f_zfs).wait_send()
+        z_low(field, 1, f_zfs).wait_send()
 
     def drain(c, carry):
         x_copy(c).wait_send()
@@ -449,6 +503,7 @@
         ]
         + [dma((chunks,))] * 7
         + [dma(())] * 7
+        + [dma((3, n_probe))] * 2
         + [dma((n_peer,)), dma((n_peer,)), dma(())]
         + [dma((n_peer,)), dma((n_peer,)), dma((n_group,)), dma((n_group,))]
         + [dma((n_peer,)), dma((n_peer,)), dma(())],
@@ -465,6 +520,14 @@
     return high, low
 
 
+def terms(values):
+    found = []
+    for _ in range(3):
+        found.append(values.astype(jnp.bfloat16).astype(jnp.float32))
+        values = values - found[-1]
+    return found
+
+
 def factor(gram_ref, work, n, rows=8):
     work[:, :n] = gram_ref[...]
     row_id = lax.broadcasted_iota(jnp.int32, (n, n), 0)
@@ -477,22 +540,31 @@
         start = pl.multiple_of(at * rows, rows)
         left = pltpu.roll(work[pl.ds(start, rows), :n], lax.rem(n - start, n), 1)
         right = work[pl.ds(start, rows), n:]
+        columns = [jnp.broadcast_to(left[:, j : j + 1], (rows, n)) for j in range(rows)]
+        pivots = columns[0]
         for j in range(rows):
-            col = jnp.broadcast_to(left[:, j : j + 1], (rows, n))
-            pivot = jnp.broadcast_to(col[j : j + 1, :], (rows, n))
-            scale = lax.rsqrt(pivot)
-            scale = scale * (1.5 - 0.5 * (pivot * scale) * scale)
-            row_left = jnp.broadcast_to(left[j : j + 1, :], (rows, n)) * scale
-            row_right = jnp.broadcast_to(right[j : j + 1, :], (rows, n)) * scale
-            times = jnp.where(sub > j, col * scale, 0.0)
-            left = jnp.where(sub == j, row_left, left - times * row_left)
-            right = jnp.where(sub == j, row_right, right - times * row_right)
-        left = pltpu.roll(left, start, 1)
+            pivot = jnp.broadcast_to(columns[j][j : j + 1, :], (rows, n))
+            times = jnp.where(sub > j, columns[j] * (1.0 / pivot), 0.0)
+            pivots = jnp.where(sub == j, pivot, pivots)
+            if j == rows - 1:
+                break
+            for i in range(j + 1, rows):
+                columns[i] -= times * jnp.broadcast_to(columns[i][j : j + 1, :], (rows, n))
+            left -= times * jnp.broadcast_to(left[j : j + 1, :], (rows, n))
+            right -= times * jnp.broadcast_to(right[j : j + 1, :], (rows, n))
+        scale = lax.rsqrt(pivots)
+        scale = scale * (1.5 - 0.5 * (pivots * scale) * scale)
+        left = pltpu.roll(left * scale, start, 1)
+        right = right * scale
         ahead = jnp.where(lane >= start + rows, left, 0.0)
         both = jnp.concatenate([left, right], axis=1)
+        a_terms, b_terms = terms(ahead), terms(both)
+        pairs = ((0, 0), (0, 1), (1, 0), (1, 1), (0, 2), (2, 0))
+        stacked_a = jnp.concatenate([a_terms[i] for i, _ in pairs], axis=0)
+        stacked_b = jnp.concatenate([b_terms[i] for _, i in pairs], axis=0)
         work[...] -= lax.dot_general(
-            ahead, both, (((0,), (0,)), ((), ())), precision=highest,
-            preferred_element_type=jnp.float32,
+            stacked_a.astype(jnp.bfloat16), stacked_b.astype(jnp.bfloat16),
+            (((0,), (0,)), ((), ())), preferred_element_type=jnp.float32,
         )
         work[pl.ds(start, rows), :] = both
         return carry

time: 163 us -> 143 us (0.88)
  Pallas kernels: 157 us -> 137 us
    pallas_call x1, Pallas kernels: 29.6 us -> 16.5 us  [basis(): pl.pallas_call(functools.partial(basis_kernel, norm_scale), out_shape=(ja...]
    pallas_call x1, Pallas kernels: 127 us -> 121 us  [exchange(): pl.pallas_call(functools.partial(exchange_kernel, n_space, n_probe, chunk...]
where the time goes in v3:
time: 143 us
  Pallas kernels  137 us (96%)
  local copies, waits for them, and re-layouts  2.55 us (2%)
  other arithmetic  2.4 us (2%)
    pallas_call x1, Pallas kernels, exchange(): pl.pallas_call(functools.partial(exchange_kernel, n_space, n_probe, chunk...  121 us
    pallas_call x1, Pallas kernels, basis(): pl.pallas_call(functools.partial(basis_kernel, norm_scale), out_shape=(ja...  16.5 us

profile of v3, /device:TPU:0, one launch (start us, length us, event | category | flops | bytes accessed | tf_op | source)
XLA Modules:
  0.0 142.8 jit_solution(13343597382188891388)
XLA Ops:
  0.6 0.0 copy-start.2
  0.6 0.0 copy-start.3
  0.7 0.7 iota_compare_fusion
  1.4 1.6 %select_reduce_fusion = f32[3,2,128,128]{3,2,1,0:T(8,128)S(1)} fusion(f32[4,3,2,128,128]{4,3,2,1,0:T(8,128)} %param.6, pred[4,2]{1,0:T(4,128)(4,1)S(1)} %iota_compare_fusion), kind=kLoop, calls=%fused_computation | loop fusion | flops 688128 | bytes 1966088 | tf_op jit(solution)/shard_map/reduce_sum | solution.py:19
  3.0 0.0 copy-done.2
  3.0 0.0 copy-done.3
  3.1 120.6 %exchange.1 = (f32[128,2,32,128]{3,2,1,0:T(8,128)S(1)}, f32[128,128]{1,0:T(8,128)S(1)}) custom-call(f32[32,2,128,128]{3,2,1,0:T(8,128)} %probes_ref.1, f32[2,5,128,128]{3,2,1,0:T(8,128)S(1)} %maximum_bitcast_fusion.fields_ref), custom_call_target="tpu_custom_call" | custom-call | tf_op jit(solution)/shard_map/exchange/pallas_call | solution.py:480
  123.7 0.0 copy-start
  123.7 1.9 %copy-done = f32[128,2,32,128]{3,2,1,0:T(8,128)} copy-done((f32[128,2,32,128]{3,2,1,0:T(8,128)}, f32[128,2,32,128]{3,2,1,0:T(8,128)S(1)}, u32[]{:S(2)}) %copy-start) | copy-done | bytes 4194328
  125.6 0.0 copy-start.1
  125.6 0.6 copy-done.1
  126.2 16.5 %basis.1 = (f32[128,64,128]{2,1,0:T(8,128)}, f32[128,128]{1,0:T(8,128)}) custom-call(f32[128,128]{1,0:T(8,128)} %copy-done.1, f32[128,64,128]{2,1,0:T(8,128)} %bitcast.6), custom_call_target="tpu_custom_call" | custom-call | tf_op jit(solution)/shard_map/basis/pallas_call | solution.py:624
  (1 shorter events, 0.0 us)
Async XLA Ops:
  0.6 2.4 %copy-start.2 = (f32[2,128,128]{2,1,0:T(8,128)S(1)}, f32[2,128,128]{2,1,0:T(8,128)}, u32[]{:S(2)}) copy-start(f32[2,128,128]{2,1,0:T(8,128)} %param.9) | copy-start | bytes 393220
  0.6 2.4 %copy-start.3 = (f32[2,128,128]{2,1,0:T(8,128)S(1)}, f32[2,128,128]{2,1,0:T(8,128)}, u32[]{:S(2)}) copy-start(f32[2,128,128]{2,1,0:T(8,128)} %param.8) | copy-start | bytes 393220
  123.7 1.9 %copy-start = (f32[128,2,32,128]{3,2,1,0:T(8,128)}, f32[128,2,32,128]{3,2,1,0:T(8,128)S(1)}, u32[]{:S(2)}) copy-start(f32[128,2,32,128]{3,2,1,0:T(8,128)S(1)} %get-tuple-element.7) | copy-start | bytes 12582916
  125.6 0.6 copy-start.1

commit v4 on v3

--- a/solution.py
+++ b/solution.py
@@ -468,7 +468,7 @@
     y_copy.wait()
 
 
-def exchange(probes, fields, n_space, n_probe, chunks=8, window=2):
+def exchange(probes, fields, n_space, n_probe, chunks=8, window=8):
     local, planes, ny, nz = probes.shape
     count = local * n_probe
     half = local // 2
@@ -508,7 +508,7 @@
         + [dma((n_peer,)), dma((n_peer,)), dma((n_group,)), dma((n_group,))]
         + [dma((n_peer,)), dma((n_peer,)), dma(())],
         compiler_params=pltpu.CompilerParams(
-            collective_id=0, has_side_effects=True, vmem_limit_bytes=48 * 1024 * 1024
+            collective_id=0, has_side_effects=True, vmem_limit_bytes=32 * 1024 * 1024
         ),
         name="exchange",
     )(probes, fields)
@@ -575,11 +575,9 @@
 
 
 def basis_kernel(
-    norm_scale, gram_ref, y_hbm, out_hbm, factor_ref, work, y_ref, out_ref, in_sem, out_sem
+    norm_scale, gram_ref, y_ref, out_hbm, factor_ref, work, out_ref, out_sem
 ):
     count, depth, nz = y_ref.shape
-    fetch = pltpu.make_async_copy(y_hbm, y_ref, in_sem)
-    fetch.start()
     upper, inverse = factor(gram_ref, work, count)
     factor_ref[...] = upper / norm_scale
     high, low = split(inverse * norm_scale)
@@ -587,7 +585,6 @@
     flat = y_ref.reshape(count * depth, nz)
     result_flat = out_ref.reshape(count * depth, nz)
     rows = 8
-    fetch.wait()
 
     def store(t):
         part = pl.ds(pl.multiple_of(t * rows, rows), rows)
@@ -627,16 +624,14 @@
             jax.ShapeDtypeStruct(y_rows.shape, f32),
             jax.ShapeDtypeStruct(gram_matrix.shape, f32),
         ),
-        in_specs=[vmem, hbm],
+        in_specs=[vmem, vmem],
         out_specs=(hbm, vmem),
         scratch_shapes=[
             pltpu.VMEM((count, 2 * count), f32),
             pltpu.VMEM(y_rows.shape, f32),
-            pltpu.VMEM(y_rows.shape, f32),
-            pltpu.SemaphoreType.DMA(()),
             pltpu.SemaphoreType.DMA((depth // 8,)),
         ],
-        compiler_params=pltpu.CompilerParams(vmem_limit_bytes=56 * 1024 * 1024),
+        compiler_params=pltpu.CompilerParams(vmem_limit_bytes=24 * 1024 * 1024),
         name="basis",
     )(gram_matrix, y_rows)
 

time: 143 us -> 138 us (0.965)
  Pallas kernels: 137 us -> 132 us
    pallas_call x1, Pallas kernels: 121 us -> 117 us  [exchange(): pl.pallas_call(functools.partial(exchange_kernel, n_space, n_probe, chunk...]
where the time goes in v4:
time: 138 us
  Pallas kernels  132 us (96%)
  other arithmetic  2.4 us (2%)
  local copies, waits for them, and re-layouts  2.19 us (2%)
    pallas_call x1, Pallas kernels, exchange(): pl.pallas_call(functools.partial(exchange_kernel, n_space, n_probe, chunk...  117 us
    pallas_call x1, Pallas kernels, basis(): pl.pallas_call(functools.partial(basis_kernel, norm_scale), out_shape=(ja...  15.7 us

profile of v4, /device:TPU:0, one launch (start us, length us, event | category | flops | bytes accessed | tf_op | source)
XLA Modules:
  0.0 137.6 jit_solution(3969086158504207807)
XLA Ops:
  0.6 0.0 copy-start.1
  0.6 0.0 copy-start.2
  0.7 0.7 iota_compare_fusion
  1.4 1.6 %select_reduce_fusion = f32[3,2,128,128]{3,2,1,0:T(8,128)S(1)} fusion(f32[4,3,2,128,128]{4,3,2,1,0:T(8,128)} %param.6, pred[4,2]{1,0:T(4,128)(4,1)S(1)} %iota_compare_fusion), kind=kLoop, calls=%fused_computation | loop fusion | flops 688128 | bytes 1966088 | tf_op jit(solution)/shard_map/reduce_sum | solution.py:19
  3.0 0.0 copy-done.1
  3.0 0.0 copy-done.2
  3.1 0.0 copy-start
  3.1 2.2 %copy-done = f32[32,2,128,128]{3,2,1,0:T(8,128)S(1)} copy-done((f32[32,2,128,128]{3,2,1,0:T(8,128)S(1)}, f32[32,2,128,128]{3,2,1,0:T(8,128)}, u32[]{:S(2)}) %copy-start) | copy-done | bytes 4194328
  5.3 116.6 %exchange.1 = (f32[128,2,32,128]{3,2,1,0:T(8,128)S(1)}, f32[128,128]{1,0:T(8,128)S(1)}) custom-call(f32[32,2,128,128]{3,2,1,0:T(8,128)S(1)} %copy-done, f32[2,5,128,128]{3,2,1,0:T(8,128)S(1)} %maximum_bitcast_fusion.fields_ref), custom_call_target="tpu_custom_call" | custom-call | tf_op jit(solution)/shard_map/exchange/pallas_call | solution.py:480
  121.9 15.7 %basis.1 = (f32[128,64,128]{2,1,0:T(8,128)}, f32[128,128]{1,0:T(8,128)}) custom-call(f32[128,128]{1,0:T(8,128)S(1)} %get-tuple-element.6.gram_ref, f32[128,64,128]{2,1,0:T(8,128)S(1)} %bitcast.6), custom_call_target="tpu_custom_call" | custom-call | tf_op jit(solution)/shard_map/basis/pallas_call | solution.py:621
  (1 shorter events, 0.0 us)
Async XLA Ops:
  0.6 2.4 %copy-start.1 = (f32[2,128,128]{2,1,0:T(8,128)S(1)}, f32[2,128,128]{2,1,0:T(8,128)}, u32[]{:S(2)}) copy-start(f32[2,128,128]{2,1,0:T(8,128)} %param.9) | copy-start | bytes 393220
  0.6 2.4 %copy-start.2 = (f32[2,128,128]{2,1,0:T(8,128)S(1)}, f32[2,128,128]{2,1,0:T(8,128)}, u32[]{:S(2)}) copy-start(f32[2,128,128]{2,1,0:T(8,128)} %param.8) | copy-start | bytes 393220
  3.1 2.2 %copy-start = (f32[32,2,128,128]{3,2,1,0:T(8,128)S(1)}, f32[32,2,128,128]{3,2,1,0:T(8,128)}, u32[]{:S(2)}) copy-start(f32[32,2,128,128]{3,2,1,0:T(8,128)} %probes_ref.1) | copy-start | bytes 12582916

commit v5 on v4

--- a/solution.py
+++ b/solution.py
@@ -468,7 +468,7 @@
     y_copy.wait()
 
 
-def exchange(probes, fields, n_space, n_probe, chunks=8, window=8):
+def exchange(probes, fields, n_space, n_probe, chunks=4, window=4):
     local, planes, ny, nz = probes.shape
     count = local * n_probe
     half = local // 2
@@ -508,7 +508,7 @@
         + [dma((n_peer,)), dma((n_peer,)), dma((n_group,)), dma((n_group,))]
         + [dma((n_peer,)), dma((n_peer,)), dma(())],
         compiler_params=pltpu.CompilerParams(
-            collective_id=0, has_side_effects=True, vmem_limit_bytes=32 * 1024 * 1024
+            collective_id=0, has_side_effects=True, vmem_limit_bytes=48 * 1024 * 1024
         ),
         name="exchange",
     )(probes, fields)

time: 138 us -> 135 us (0.978)
  local copies, waits for them, and re-layouts: 2.19 us -> 0.01 us
    unnamed x6 -> x4, local copies, waits for them, and re-layouts: 2.19 us -> 0.01 us
where the time goes in v5:
time: 135 us
  Pallas kernels  132 us (98%)
  other arithmetic  2.4 us (2%)
    pallas_call x1, Pallas kernels, exchange(): pl.pallas_call(functools.partial(exchange_kernel, n_space, n_probe, chunk...  116 us
    pallas_call x1, Pallas kernels, basis(): pl.pallas_call(functools.partial(basis_kernel, norm_scale), out_shape=(ja...  15.7 us

profile of v5, /device:TPU:0, one launch (start us, length us, event | category | flops | bytes accessed | tf_op | source)
XLA Modules:
  0.0 134.9 jit_solution(9911333259741552802)
XLA Ops:
  0.6 0.0 copy-start
  0.6 0.0 copy-start.1
  0.7 0.7 iota_compare_fusion
  1.4 1.6 %select_reduce_fusion = f32[3,2,128,128]{3,2,1,0:T(8,128)S(1)} fusion(f32[4,3,2,128,128]{4,3,2,1,0:T(8,128)} %param.6, pred[4,2]{1,0:T(4,128)(4,1)S(1)} %iota_compare_fusion), kind=kLoop, calls=%fused_computation | loop fusion | flops 688128 | bytes 1966088 | tf_op jit(solution)/shard_map/reduce_sum | solution.py:19
  3.0 0.0 copy-done
  3.0 0.0 copy-done.1
  3.1 116.1 %exchange.1 = (f32[128,2,32,128]{3,2,1,0:T(8,128)S(1)}, f32[128,128]{1,0:T(8,128)S(1)}) custom-call(f32[32,2,128,128]{3,2,1,0:T(8,128)} %probes_ref.1, f32[2,5,128,128]{3,2,1,0:T(8,128)S(1)} %maximum_bitcast_fusion.fields_ref), custom_call_target="tpu_custom_call" | custom-call | tf_op jit(solution)/shard_map/exchange/pallas_call | solution.py:480
  119.2 15.7 %basis.1 = (f32[128,64,128]{2,1,0:T(8,128)}, f32[128,128]{1,0:T(8,128)}) custom-call(f32[128,128]{1,0:T(8,128)S(1)} %get-tuple-element.6.gram_ref, f32[128,64,128]{2,1,0:T(8,128)S(1)} %bitcast.6), custom_call_target="tpu_custom_call" | custom-call | tf_op jit(solution)/shard_map/basis/pallas_call | solution.py:621
  (1 shorter events, 0.0 us)
Async XLA Ops:
  0.6 2.4 %copy-start = (f32[2,128,128]{2,1,0:T(8,128)S(1)}, f32[2,128,128]{2,1,0:T(8,128)}, u32[]{:S(2)}) copy-start(f32[2,128,128]{2,1,0:T(8,128)} %param.9) | copy-start | bytes 393220
  0.6 2.4 %copy-start.1 = (f32[2,128,128]{2,1,0:T(8,128)S(1)}, f32[2,128,128]{2,1,0:T(8,128)}, u32[]{:S(2)}) copy-start(f32[2,128,128]{2,1,0:T(8,128)} %param.8) | copy-start | bytes 393220

commit v6 on v5

--- a/solution.py
+++ b/solution.py
@@ -365,7 +365,7 @@
         )
         return carry
 
-    lax.fori_loop(0, depth // 8, gram_step, 0)
+    lax.fori_loop(0, depth // 8, gram_step, 0, unroll=2)
     across = gram_acc[:count, count:] + gram_acc[count:, :count]
     gram_part[...] = gram_acc[:count, :count] + (across + gram_acc[count:, count:])
 
@@ -604,7 +604,7 @@
         store(t).start()
         return carry
 
-    lax.fori_loop(0, depth // rows, block_step, 0)
+    lax.fori_loop(0, depth // rows, block_step, 0, unroll=2)
 
     def drain(t, carry):
         store(t).wait()

time: 135 us -> 134 us (level)
  no operation moved by 1% of the time
where the time goes in v6:
time: 134 us
  Pallas kernels  131 us (98%)
  other arithmetic  2.4 us (2%)
    pallas_call x1, Pallas kernels, exchange(): pl.pallas_call(functools.partial(exchange_kernel, n_space, n_probe, chunk...  115 us
    pallas_call x1, Pallas kernels, basis(): pl.pallas_call(functools.partial(basis_kernel, norm_scale), out_shape=(ja...  15.3 us

profile of v6, /device:TPU:0, one launch (start us, length us, event | category | flops | bytes accessed | tf_op | source)
XLA Modules:
  0.0 133.8 jit_solution(6362399493519780513)
XLA Ops:
  0.6 0.0 copy-start
  0.6 0.0 copy-start.1
  0.7 0.7 iota_compare_fusion
  1.4 1.6 %select_reduce_fusion = f32[3,2,128,128]{3,2,1,0:T(8,128)S(1)} fusion(f32[4,3,2,128,128]{4,3,2,1,0:T(8,128)} %param.6, pred[4,2]{1,0:T(4,128)(4,1)S(1)} %iota_compare_fusion), kind=kLoop, calls=%fused_computation | loop fusion | flops 688128 | bytes 1966088 | tf_op jit(solution)/shard_map/reduce_sum | solution.py:19
  3.0 0.0 copy-done
  3.0 0.0 copy-done.1
  3.1 115.3 %exchange.1 = (f32[128,2,32,128]{3,2,1,0:T(8,128)S(1)}, f32[128,128]{1,0:T(8,128)S(1)}) custom-call(f32[32,2,128,128]{3,2,1,0:T(8,128)} %probes_ref.1, f32[2,5,128,128]{3,2,1,0:T(8,128)S(1)} %maximum_bitcast_fusion.fields_ref), custom_call_target="tpu_custom_call" | custom-call | tf_op jit(solution)/shard_map/exchange/pallas_call | solution.py:480
  118.4 15.3 %basis.1 = (f32[128,64,128]{2,1,0:T(8,128)}, f32[128,128]{1,0:T(8,128)}) custom-call(f32[128,128]{1,0:T(8,128)S(1)} %get-tuple-element.6.gram_ref, f32[128,64,128]{2,1,0:T(8,128)S(1)} %bitcast.6), custom_call_target="tpu_custom_call" | custom-call | tf_op jit(solution)/shard_map/basis/pallas_call | solution.py:621
  (1 shorter events, 0.0 us)
Async XLA Ops:
  0.6 2.4 %copy-start = (f32[2,128,128]{2,1,0:T(8,128)S(1)}, f32[2,128,128]{2,1,0:T(8,128)}, u32[]{:S(2)}) copy-start(f32[2,128,128]{2,1,0:T(8,128)} %param.9) | copy-start | bytes 393220
  0.6 2.4 %copy-start.1 = (f32[2,128,128]{2,1,0:T(8,128)S(1)}, f32[2,128,128]{2,1,0:T(8,128)}, u32[]{:S(2)}) copy-start(f32[2,128,128]{2,1,0:T(8,128)} %param.8) | copy-start | bytes 393220
